TPU v7x, 32 devices: a whole 2x2x4 slice. The times are simulated.
32 devices in a mesh: dp: 8 (over y, x, core), shard: 4 (over z).
Axes of the slice: x: 2, y: 2, z: 4, core: 2. Of those that a mesh axis runs over, the one named last changes fastest.
Arguments:
- features: bfloat16 [65536, 2048], P(('dp', 'shard')), may hold values from -6 to 6
- neighbors: int32 [65536, 128], P(('dp', 'shard')), may hold values from -1 to 1023, as said below
- weight: bfloat16 [2048, 2048], P(('dp', 'shard')), may hold values from -0.125 to 0.125
- bias_terms: bfloat16 [2048], P(('dp', 'shard')), may hold values from -1.796875 to 1.796875
- grad_out: bfloat16 [65536, 2048], P(('dp', 'shard')), may hold values from -6 to 6
Outputs:
- activations: bfloat16 [65536, 2048], P(('dp', 'shard'))
- grad_features: float32 [65536, 2048], P(('dp', 'shard'))
- grad_weight: float32 [2048, 2048], P(('dp', 'shard'))
- grad_bias: float32 [2048], P(('dp', 'shard'))
Inputs may be any that keep to these rules, and one draw needn't show every extreme that they name: `neighbors`: each row lists neighbours of its node as indices within its cluster (clusters are aligned blocks of 1024 rows): used slots first, then -1 pads. An index may repeat; each slot counts as one edge. Every row has at least one neighbour, and the first row of every cluster uses all 128 slots.
All inputs are finite; a program needn't handle non-finite values.
Results may differ from a plain program's by a relative error of at most 0.0057.
Values may be sent and summed in bfloat16 or wider, within the bound.
A program may use at most 192 MiB of HBM per device.

v0:
```python
import jax
import jax.numpy as jnp
from jax import lax
from jax.experimental import pallas as pl
from jax.experimental.pallas import tpu as pltpu
from jax.sharding import PartitionSpec as P

F32, BF16, I32 = jnp.float32, jnp.bfloat16, jnp.int32
MESH = pl.DeviceIdType.MESH
CLUSTER = 1024
SLOTS = 128
UNROLL = 32
LOW = 64
PC = 512
HC = 256
ALPHA = 0.7978845608028654
BETA = ALPHA * 0.044715
NN = (((1,), (0,)), ((), ()))
TN = (((0,), (0,)), ((), ()))
NT = (((1,), (1,)), ((), ()))
ALL = slice(None)

GATHER = ("zxy", "zyx", "zxy", "zyx", "zxy", "zyx", "xzy", "yzx")
SCATTER = ("yzx", "xzy", "yxz", "xyz", "yxz", "xyz", "yxz", "xyz")
COUNT_EVENTS = (
    (4, "second", 0),
    (6, "first", 2),
    (8, "third", 0),
    (8, "second", 1),
    (12, "second", 3),
    (12, "second", 2),
)
MIX_EVENTS = (
    (0, "third", 1),
    (0, "pass", 0),
    (3, "third", 2),
    (7, "third", 3),
    (7, "pass", 1),
)
PANEL_GATHER = (
    (0, "ready", 1),
    (1, "pass", 2),
    (4, "pass", 3),
    (4, "ready", 2),
    (8, "ready", 3),
)
PANEL_SCATTER = (
    (7, 1, 0),
    (11, 1, 1),
    (13, 2, 0),
    (14, 2, 1),
    (15, 1, 2),
)
BACK_SCATTER = (
    (0, 3, 0),
    (1, 3, 1),
    (1, 2, 2),
    (3, 1, 3),
    (3, 3, 2),
    (5, 2, 3),
)


def dot(a, b, dims):
    return lax.dot_general(a, b, dims, preferred_element_type=F32)


class Place:
    def __init__(self, dp_size, shard_size):
        dp, self.z = lax.axis_index("dp"), lax.axis_index("shard")
        self.dp = dp
        self.c, self.x, self.y = dp % 2, (dp // 2) % 2, dp // 4
        self.size = {"c": 2, "x": 2, "y": dp_size // 4, "z": shard_size}

    def at(self, dim):
        return {"c": self.c, "x": self.x, "y": self.y, "z": self.z}[dim]

    def shifted(self, dim, offset):
        size = self.size[dim]
        return lax.rem(self.at(dim) + (offset + size), size)

    def peer(self, dim, offset):
        other = self.shifted(dim, offset)
        if dim == "z":
            return (self.dp, other)
        step = {"c": 1, "x": 2, "y": 4}[dim]
        return (self.dp + step * (other - self.at(dim)), self.z)

    def lane(self, rows):
        return (self.dp * self.size["z"] + self.z) * rows % 128

    def offsets(self, dim):
        return range(1, self.size[dim])


class Sems:
    def __init__(self):
        self.index = {}

    def __getitem__(self, name):
        return self.index.setdefault(name, len(self.index))


def sem_names(sizes):
    sems = Sems()
    for t in list(range(len(GATHER))) + ["bias"]:
        path = GATHER[0] if t == "bias" else GATHER[t]
        for k in range(3):
            for o in range(1, sizes[path[k]]):
                sems["gather", t, k, o]
        sems["core", t, 0]
        for o in range(1, sizes[path[2]]):
            sems["core", t, o]
    for t in list(range(len(SCATTER))) + ["bias"]:
        path = SCATTER[0] if t == "bias" else SCATTER[t]
        for k in range(3):
            for o in range(1, sizes[path[k]]):
                for h in range(2 if k == 0 and path[0] == "x" else 1):
                    sems["scatter", t, k, o, h]
    sems["swap", "bias"]
    for s in range(len(SCATTER)):
        sems["swap", s]
    return sems


def linkable(rows):
    return rows % 16 == 0


def make_kernel(dp_size, shard_size, rows, width, nodes):
    sizes = {"c": 2, "x": 2, "y": dp_size // 4, "z": shard_size}
    Y, X, S, R = sizes["y"], 2, shard_size, rows
    SR = S * R
    n_dev = dp_size * shard_size
    panels = width // PC
    half_rows = width // 2
    clusters = nodes // CLUSTER
    sems = sem_names(sizes)
    n_sems = len(sems.index)
    chunks = nodes // 128
    TM = 512
    tiles = (nodes // TM) * panels
    per_panel = nodes // TM
    BM = 256

    def stage_shape(path, k):
        n = sizes[path[k]] - 1
        left = path[k + 1 :]
        lead = tuple(sizes[d] for d in "yx" if d in left)
        return (n,) + lead, ("z" in left)

    def stage_shapes():
        out = []
        for t in range(len(SCATTER)):
            for k in range(3):
                lead, z = stage_shape(SCATTER[t], k)
                out.append(pltpu.VMEM(lead + (SR if z else R, HC), BF16))
        for k in range(3):
            lead, z = stage_shape(SCATTER[0], k)
            out.append(pltpu.VMEM(lead + (S if z else 1, 8, 128), F32))
        return out

    n_stage = 3 * (len(SCATTER) + 1)
    linked = linkable(rows)

    def kernel(
        f_hbm, n_hbm, w_hbm, b_in, g_hbm,
        act_hbm, fg, a2t, gw_out, gb_out,
        mixed, wg, fac, b_own, bt, brow, gbacc, cr, crb, ptb, *rest,
    ):
        stage = rest[:n_stage]
        ssem, rsem, lsem = rest[n_stage:]
        me = Place(dp_size, shard_size)
        c, x, y, z = me.c, me.x, me.y, me.z
        started = {}

        def remote(name, src, dst, device):
            i = sems[name]
            return pltpu.make_async_remote_copy(
                src_ref=src, dst_ref=dst, send_sem=ssem.at[i], recv_sem=rsem.at[i],
                device_id=device, device_id_type=MESH,
            )

        def send(name, make):
            remote(name, *make()).start()
            started[name] = make

        def arrived(name, ref):
            remote(name, ref, ref, me.peer("c", 1)).wait_recv()

        def view(t, core, **at):
            ys, xs = at.get("y", ALL), at.get("x", ALL)
            if t == "bias":
                zs = pl.ds(at["z"], 1) if "z" in at else ALL
                return bt.at[ys, xs, core, zs]
            zs = pl.ds(pl.multiple_of(at["z"] * R, R), R) if "z" in at else ALL
            return wg.at[t // 2, ys, xs, core, zs, pl.ds(t % 2 * HC, HC)]

        own = {"x": x, "y": y, "z": z}

        def fixed(dims):
            return {d: own[d] for d in dims}

        def gather_path(t):
            return GATHER[0] if t == "bias" else GATHER[t]

        def gather_first(t):
            path = gather_path(t)

            def make(o):
                if t == "bias":
                    return b_own, bt.at[y, x, c, z], me.peer(path[0], o)
                src = w_hbm.at[:, pl.ds(t * HC, HC)]
                return src, view(t, c, **fixed("xyz")), me.peer(path[0], o)

            for o in me.offsets(path[0]):
                send(("gather", t, 0, o), lambda o=o: make(o))

        def gather_wait(t, k):
            path = gather_path(t)
            for o in me.offsets(path[k]):
                at = fixed(path[k:])
                at[path[k]] = me.shifted(path[k], -o)
                arrived(("gather", t, k, o), view(t, c, **at))

        def gather_send(t, k):
            path = gather_path(t)

            def make(o):
                ref = view(t, c, **fixed(path[k:]))
                return ref, ref, me.peer(path[k], o)

            for o in me.offsets(path[k]):
                send(("gather", t, k, o), lambda o=o: make(o))

        def core_send(t, late):
            path = gather_path(t)

            def make(o):
                at = {path[2]: me.shifted(path[2], -o)} if o else fixed(path[2:])
                ref = view(t, c, **at)
                return ref, ref, me.peer("c", 1)

            for o in me.offsets(path[2]) if late else (0,):
                send(("core", t, o), lambda o=o: make(o))

        def core_wait(t):
            path = gather_path(t)
            arrived(("core", t, 0), view(t, 1 - c, **fixed(path[2:])))
            for o in me.offsets(path[2]):
                arrived(
                    ("core", t, o),
                    view(t, 1 - c, **{path[2]: me.shifted(path[2], -o)}),
                )

        def slices(panel):
            return (2 * panel, 2 * panel + 1) + (("bias",) if panel == 0 else ())

        def own_block(j):
            if not linked:
                return pltpu.make_async_copy(
                    w_hbm.at[:, :, :, :, pl.ds(j * PC, PC)], wg.at[j], lsem.at[8 + j]
                )
            return pltpu.make_async_copy(
                w_hbm.at[:, pl.ds(j * PC, PC)],
                wg.at[j, y, x, c, pl.ds(pl.multiple_of(z * R, R), R), :],
                lsem.at[8 + j],
            )

        def own_bias():
            return pltpu.make_async_copy(b_own, bt.at[y, x, c, z], lsem.at[8 + panels])

        def gather_event(kind, panel):
            if not linked:
                if kind == "ready":
                    own_block(panel).wait()
            elif kind == "first":
                for t in slices(panel):
                    gather_first(t)
            elif kind == "second":
                for t in slices(panel):
                    gather_wait(t, 0)
                own_block(panel).wait()
                if panel == 0:
                    own_bias().wait()
                for t in slices(panel):
                    gather_send(t, 1)
            elif kind == "third":
                for t in slices(panel):
                    gather_wait(t, 1)
                for t in slices(panel):
                    gather_send(t, 2)
                for t in slices(panel):
                    core_send(t, False)
            elif kind == "pass":
                for t in slices(panel):
                    gather_wait(t, 2)
                for t in slices(panel):
                    core_send(t, True)
            elif kind == "ready":
                for t in slices(panel):
                    core_wait(t)

        load_n = lambda ref: pltpu.make_async_copy(n_hbm, ref, lsem.at[9 + panels])
        load_f = pltpu.make_async_copy(f_hbm, fg, lsem.at[10 + panels])

        def count_phase(nb, low, *digits):
            load_n(nb).start()
            peers = [me.peer(d, o) for d in "cxyz" for o in me.offsets(d) if linked]
            for p in peers:
                pl.semaphore_signal(
                    pltpu.get_barrier_semaphore(), inc=1,
                    device_id=p, device_id_type=MESH,
                )
            for j in range(panels):
                own_block(j).start()
            if linked:
                bias = b_in[...].astype(F32)
                bias = jnp.concatenate([bias, jnp.zeros((1, 128 - R), F32)], axis=1)
                bias = jnp.broadcast_to(bias, (8, 128))
                b_own[...] = pltpu.roll(bias, me.lane(R), 1)
                own_bias().start()
                pl.semaphore_wait(pltpu.get_barrier_semaphore(), len(peers))
            gather_event("first", 0)
            gather_event("first", 3)
            load_f.start()
            load_n(nb).wait()

            @pl.loop(0, chunks)
            def _(q):
                r = pl.ds(pl.multiple_of(q * 128, 128), 128)
                ids = nb[r, :]
                degree = jnp.sum((ids >= 0).astype(F32), axis=1, keepdims=True)
                fac[r, :] = jnp.broadcast_to(1.0 / (degree + 1.0), (128, 128))
                ids = ids.T
                high = ids >> (LOW.bit_length() - 1)
                digit = jnp.left_shift(jnp.ones_like(ids), (high & 3) * 8)
                low[:, r] = ids & (LOW - 1)
                for k, ref in enumerate(digits):
                    ref[:, r] = jnp.where(high >> 2 == k, digit, 0)

            gather_event("first", 1)
            place_in = lax.broadcasted_iota(I32, (LOW, 128), 0)
            lane = lax.broadcasted_iota(I32, (LOW, 128), 1)

            @pl.loop(0, chunks)
            def _(q):
                col = pl.ds(pl.multiple_of(q * 128, 128), 128)

                def step(s, carry):
                    some = pl.ds(pl.multiple_of(s * UNROLL, UNROLL), UNROLL)
                    lo, add = low[some, col], [ref[some, col] for ref in digits]
                    for k in range(UNROLL):
                        hit = lo[k : k + 1] == place_in
                        carry = tuple(
                            total + jnp.where(hit, a[k : k + 1], 0)
                            for total, a in zip(carry, add)
                        )
                    return carry

                zero = (jnp.zeros((LOW, 128), I32),) * len(digits)
                totals = lax.fori_loop(0, SLOTS // UNROLL, step, zero)
                cl, place = q // 8, q % 8
                to = pl.ds(pl.multiple_of(place * 128, 128), 128)
                for b in range(CLUSTER // LOW):
                    count = ((totals[b // 4] >> (8 * (b % 4))) & 255).astype(F32)
                    self_at = place * 128 - b * LOW
                    count = count + jnp.where(place_in - lane == self_at, 2.0, 0.0)
                    a2t[cl, pl.ds(b * LOW, LOW), to] = count.astype(BF16)
                for at, kind, panel in COUNT_EVENTS:
                    pl.when(q == at)(lambda k=kind, p=panel: gather_event(k, p))

        pl.run_scoped(
            count_phase,
            pltpu.VMEM((nodes, SLOTS), I32),
            *[pltpu.VMEM((SLOTS, nodes), I32)] * (1 + CLUSTER // LOW // 4),
        )
        load_f.wait()

        @pl.loop(0, clusters * 4)
        def _(s):
            cl, i, j = s // 4, (s // 2) % 2, s % 2
            r = pl.ds(pl.multiple_of(cl * CLUSTER + i * 512, 512), 512)
            k = pl.ds(pl.multiple_of(cl * CLUSTER, CLUSTER), CLUSTER)
            col = pl.ds(pl.multiple_of(j * half_rows, half_rows), half_rows)
            links = a2t[cl, :, pl.ds(pl.multiple_of(i * 512, 512), 512)]
            total = dot(links, fg[k, col], TN)
            scale = jnp.concatenate([fac[r, :]] * (half_rows // 128), axis=1)
            mixed[r, col] = (scale * total).astype(BF16)
            for at, kind, panel in MIX_EVENTS:
                pl.when(s == at)(lambda k=kind, p=panel: gather_event(k, p))

        half_y = Y // 2
        y_half = y // half_y

        def half_of(hh):
            if isinstance(hh, int):
                return y_half if hh else 1 - y_half
            return jnp.where(hh == 0, 1 - y_half, y_half)

        def part(pt, t, core, **at):
            ys, xs = at.get("y", ALL), at.get("x", ALL)
            if t == "bias":
                zs = pl.ds(at["z"], 1) if "z" in at else ALL
                return ptb.at[ys, xs, core, zs]
            zs = pl.ds(pl.multiple_of(at["z"] * R, R), R) if "z" in at else ALL
            return pt.at[t // 2, ys, xs, core, zs, pl.ds(t % 2 * HC, HC)]

        def scatter_path(t):
            return SCATTER[0] if t == "bias" else SCATTER[t]

        def landing(t, k):
            return stage[(len(SCATTER) if t == "bias" else t) * 3 + k]

        def scatter_send(pt, t, k, h=None):
            path = scatter_path(t)

            def make(o):
                at = fixed(path[:k])
                at[path[k]] = me.shifted(path[k], o)
                dst = landing(t, k).at[o - 1]
                if h is not None:
                    ys = pl.ds(half_of(h) * half_y, half_y)
                    at["y"] = ys
                    dst = dst.at[ys]
                return part(pt, t, c, **at), dst, me.peer(path[k], o)

            for o in me.offsets(path[k]):
                send(("scatter", t, k, o, h or 0), lambda o=o: make(o))

        def scatter_wait(t, k):
            path = scatter_path(t)
            for o in me.offsets(path[k]):
                ref = landing(t, k).at[o - 1]
                if t != "bias" and k == 0 and path[0] == "x":
                    for i in range(2):
                        ys = pl.ds(half_of(i) * half_y, half_y)
                        arrived(("scatter", t, k, o, i), ref.at[ys])
                else:
                    arrived(("scatter", t, k, o, 0), ref)

        def over_rows(shape, action):
            lead, high = shape[:-2], shape[-2]
            step = min(high, 64)

            def walk(index):
                if len(index) < len(lead):
                    if lead[len(index)] == 1:
                        walk(index + (0,))
                    else:
                        pl.loop(0, lead[len(index)])(lambda k: walk(index + (k,)))
                elif high == step:
                    action(index + (pl.ds(0, step),))
                else:
                    pl.loop(0, high // step)(
                        lambda k: action(
                            index + (pl.ds(pl.multiple_of(k * step, step), step),)
                        )
                    )

            walk(())

        def scatter_add(pt, t, k):
            path = scatter_path(t)
            mine = part(pt, t, c, **fixed(path[: k + 1]))
            others = [landing(t, k).at[o - 1] for o in me.offsets(path[k])]
            if t == "bias":
                total = mine[...]
                for other in others:
                    total = total + other[...]
                if k < 2:
                    mine[...] = total
                else:
                    gb_out[...] = total.reshape(8, 128)
                return

            def piece(at):
                total = mine[at].astype(F32)
                for other in others:
                    total = total + other[at].astype(F32)
                if k < 2:
                    mine[at] = total.astype(BF16)
                else:
                    gw_out[at[0], pl.ds(t * HC, HC)] = total

            over_rows(mine.shape, piece)

        def swap(pt, s):
            j, hh = s // 2, s % 2
            ys = pl.ds(half_of(hh) * half_y, half_y)
            i = sems["swap", 0] + s
            return pltpu.make_async_remote_copy(
                src_ref=pt.at[j, ys, :, 1 - c], dst_ref=cr.at[j, ys],
                send_sem=ssem.at[i], recv_sem=rsem.at[i],
                device_id=me.peer("c", 1), device_id_type=MESH,
            )

        def core_sum(pt, s):
            swap(pt, s).wait_recv()
            ys = pl.ds(half_of(s % 2) * half_y, half_y)
            mine, other = pt.at[s // 2, ys, :, c], cr.at[s // 2, ys]

            def piece(at):
                mine[at] = (mine[at].astype(F32) + other[at].astype(F32)).astype(BF16)

            over_rows(mine.shape, piece)

        def first_sends(pt, s):
            j, hh = s // 2, s % 2
            for t in (2 * j, 2 * j + 1):
                if scatter_path(t)[0] == "x":
                    scatter_send(pt, t, 0, hh)
                elif hh == (0 if Y == 2 else 1):
                    scatter_send(pt, t, 0)

        def scatter_event(pt, k, j):
            ts = (2 * j, 2 * j + 1) + (("bias",) if j == panels - 1 else ())
            for t in ts:
                scatter_wait(t, k - 1)
                scatter_add(pt, t, k - 1)
                if k < 3:
                    scatter_send(pt, t, k)

        def store_part(pt, s):
            j, hh = s // 2, s % 2
            ys = pl.ds(half_of(hh) * half_y, half_y)
            return pltpu.make_async_copy(
                pt.at[j, ys],
                gw_out.at[ys, :, :, :, pl.ds(pl.multiple_of(j * PC, PC), PC)],
                lsem.at[12 + panels + s],
            )

        def panel_phase(pt, acc_a, acc_b, go, ac):
            def tile_rows(i):
                return pl.ds(pl.multiple_of(i * TM, TM), TM)

            def block(hbm, j, i):
                return hbm.at[tile_rows(i), pl.ds(pl.multiple_of(j * PC, PC), PC)]

            def load_g(j, i):
                return pltpu.make_async_copy(block(g_hbm, j, i), go.at[i], lsem.at[i])

            def store_act(j, i):
                return pltpu.make_async_copy(
                    ac.at[i], block(act_hbm, j, i), lsem.at[4 + i]
                )

            def product(j, i):
                panel = wg[j].reshape(width, PC)
                return dot(mixed[tile_rows(i), :], panel, NN)

            def finish(acc, j, i):
                r = tile_rows(i)
                col = pl.ds(pl.multiple_of(j * PC, PC), PC)
                v = acc[...] + brow[0:1, col]
                u = v * v
                h = 0.5 + 0.5 * jnp.tanh(v * (ALPHA + BETA * u))
                a = v * h
                d = h + (a * (1.0 - h)) * (2 * ALPHA + (6 * BETA) * u)
                g = go[i].astype(F32) * d
                ac[i] = a.astype(BF16)
                fg[r, col] = g.astype(BF16)
                gbacc[:, col] += jnp.sum(g.reshape(TM // 8, 8, PC), axis=0)

            def weight_tile(j, hh):
                h = half_of(hh)
                rows_ = pl.ds(pl.multiple_of(h * half_rows, half_rows), half_rows)
                col = pl.ds(pl.multiple_of(j * PC, PC), PC)
                total = dot(mixed[:, rows_], fg[:, col], TN).astype(BF16)
                pt[j, pl.ds(h * half_y, half_y)] = total.reshape(half_y, X, 2, SR, PC)

            def leave(j, hh):
                if linked:
                    swap(pt, 2 * j + hh).start()
                else:
                    store_part(pt, 2 * j + hh).start()

            def events(step):
                for at, kind, panel in PANEL_GATHER:
                    pl.when(step == at)(lambda k=kind, p=panel: gather_event(k, p))
                if not linked:
                    return
                for at, k, panel in PANEL_SCATTER:
                    pl.when(step == at)(lambda k=k, p=panel: scatter_event(pt, k, p))

            def core_step(e, when):
                if not linked:
                    return

                @pl.when(when)
                def _():
                    core_sum(pt, e)
                    for fixed_e in range(2 * panels - 1):
                        pl.when(e == fixed_e)(lambda k=fixed_e: first_sends(pt, k))

            def send_bias():
                for d in range(n_dev):
                    col = pl.ds(d * R // 128 * 128, 128)
                    at = (d // (X * 2 * S), d // (2 * S) % X, d // S % 2, d % S)
                    ptb[at] = gbacc[:, col]
                send(
                    ("swap", "bias"),
                    lambda: (ptb.at[:, :, 1 - c], crb, me.peer("c", 1)),
                )

            def sum_bias():
                arrived(("swap", "bias"), crb)
                mine = ptb.at[:, :, c]
                mine[...] = mine[...] + crb[...]
                scatter_send(pt, "bias", 0)

            def panel(j):
                final = panels - 1

                @pl.loop(0, per_panel // 2)
                def _(h):
                    for k, acc, other in ((0, acc_a, acc_b), (1, acc_b, acc_a)):
                        i = 2 * h + k
                        load_g(j, i).wait()
                        pl.when(j > 0)(lambda i=i: store_act(j - 1, i).wait())
                    for k, acc, other in ((0, acc_a, acc_b), (1, acc_b, acc_a)):
                        i = 2 * h + k
                        n = jnp.minimum(j * per_panel + i + 1, tiles - 1)
                        other[...] = product(n // per_panel, n % per_panel)
                        finish(acc, j, i)
                    for k in range(2):
                        i = 2 * h + k
                        store_act(j, i).start()
                        pl.when(j < final)(lambda i=i: load_g(j + 1, i).start())
                    core_step(2 * j - 1, (h == 0) & (j > 0))
                    events(4 * j + h)

                @pl.loop(0, 2)
                def _(hh):
                    if linked:
                        pl.when((j == final) & (hh == 0))(send_bias)
                    weight_tile(j, hh)
                    leave(j, hh)
                    if linked:
                        pl.when((j == final) & (hh == 1))(sum_bias)
                    core_step(2 * j, hh == 1)
                    events(4 * j + 2 + hh)

            for i in range(per_panel):
                load_g(0, i).start()
            gather_event("ready", 0)
            p = 128 // R
            if not linked:
                brow[...] = b_in[...]
            for k in range(width // 128 if linked else 0):
                tile = jnp.zeros((8, 128), F32)
                for d in range(k * p, (k + 1) * p):
                    tile = tile + bt[d // (X * 2 * S), d // (2 * S) % X, d // S % 2, d % S]
                brow[:, pl.ds(k * 128, 128)] = tile
            gbacc[...] = jnp.zeros_like(gbacc)
            acc_a[...] = product(0, 0)
            pl.loop(0, panels)(panel)
            for i in range(per_panel):
                store_act(panels - 1, i).wait()

        def back_phase(pt):
            steps = nodes // BM

            @pl.loop(0, steps)
            def _(s):
                r = pl.ds(pl.multiple_of(s * BM, BM), BM)
                total = None
                for j in range(panels):
                    rhs = wg[j].reshape(width, PC)
                    term = dot(fg[r, pl.ds(j * PC, PC)], rhs, NT)
                    total = term if total is None else total + term
                scale = jnp.concatenate([fac[r, :]] * (width // 128), axis=1)
                fg[r, :] = (scale * total).astype(BF16)
                if not linked:
                    return

                @pl.when(s == 0)
                def _():
                    core_sum(pt, 2 * panels - 1)
                    first_sends(pt, 2 * panels - 1)

                for at, k, panel in BACK_SCATTER:
                    pl.when(s == at)(lambda k=k, p=panel: scatter_event(pt, k, p))

            if linked:
                scatter_event(pt, 3, panels - 1)
                for s in range(2 * panels):
                    swap(pt, s).wait_send()
                for name, make in started.items():
                    remote(name, *make()).wait_send()
            else:
                for s in range(2 * panels):
                    store_part(pt, s).wait()
                gb_out[...] = gbacc[...]

        def with_parts(pt):
            pl.run_scoped(
                lambda *refs: panel_phase(pt, *refs),
                *[pltpu.VMEM((TM, PC), F32)] * 2,
                *[pltpu.VMEM((per_panel, TM, PC), BF16)] * 2,
            )
            back_phase(pt)

        pl.run_scoped(with_parts, pltpu.VMEM((panels, Y, X, 2, SR, PC), BF16))

    away = pl.BlockSpec(memory_space=pltpu.HBM)
    here = pl.BlockSpec(memory_space=pltpu.VMEM)
    scratch = [
        pltpu.VMEM((nodes, width), BF16),
        pltpu.VMEM((panels, Y, X, 2, SR, PC), BF16),
        pltpu.VMEM((nodes, 128), F32),
        pltpu.VMEM((8, 128), F32),
        pltpu.VMEM((Y, X, 2, S, 8, 128), F32),
        pltpu.VMEM((8, width), F32),
        pltpu.VMEM((8, width), F32),
        pltpu.VMEM((panels, Y, X, SR, PC), BF16),
        pltpu.VMEM((Y, X, S, 8, 128), F32),
        pltpu.VMEM((Y, X, 2, S, 8, 128), F32),
        *stage_shapes(),
        pltpu.SemaphoreType.DMA((n_sems,)),
        pltpu.SemaphoreType.DMA((n_sems,)),
        pltpu.SemaphoreType.DMA((12 + 3 * panels,)),
    ]
    if not linked:
        for k in (3, 4, 7, 8, 9, *range(10, 10 + n_stage)):
            scratch[k] = pltpu.VMEM((8, 128), F32)
        scratch[-3] = scratch[-2] = pltpu.SemaphoreType.DMA((1,))
    return pl.pallas_call(
        kernel,
        out_shape=(
            jax.ShapeDtypeStruct((nodes, width), BF16),
            pltpu.VMEM((nodes, width), BF16),
            pltpu.VMEM((clusters, CLUSTER, CLUSTER), BF16),
            pltpu.VMEM((R, width), F32)
            if linked
            else jax.ShapeDtypeStruct((Y, X, 2, SR, width), BF16),
            pltpu.VMEM((8, 128 if linked else width), F32),
        ),
        in_specs=[away] * 3 + [here, away],
        out_specs=(away, here, here, here if linked else away, here),
        scratch_shapes=scratch,
        compiler_params=pltpu.CompilerParams(
            collective_id=0 if linked else None,
            has_side_effects=True,
            vmem_limit_bytes=48 * 2**20,
        ),
        name="layer",
    )


def make_last(dp_size, shard_size, rows, width, nodes):
    clusters = nodes // CLUSTER
    per_cluster = width // PC
    steps = clusters * per_cluster
    part_rows = nodes // steps
    linked = linkable(rows)

    def kernel(links, spread, act_in, gw_in, gb_in, out, act_out, gw_out, gb_out, held, tiles, sem):
        def inward(k):
            part = act_in.at[pl.ds(pl.multiple_of(k * part_rows, part_rows), part_rows)]
            return pltpu.make_async_copy(part, held.at[k], sem.at[k])

        def outward(k):
            part = act_out.at[pl.ds(pl.multiple_of(k * part_rows, part_rows), part_rows)]
            return pltpu.make_async_copy(held.at[k], part, sem.at[steps + k])

        def place(k):
            return (
                pl.ds(pl.multiple_of(k // per_cluster * CLUSTER, CLUSTER), CLUSTER),
                pl.ds(pl.multiple_of(k % per_cluster * PC, PC), PC),
            )

        def store(k):
            return pltpu.make_async_copy(
                tiles.at[k % 2], out.at[place(k)], sem.at[2 * steps + k % 2]
            )

        carry = pltpu.make_async_copy(gw_in, gw_out, sem.at[2 * steps + 2])
        @pl.loop(0, steps)
        def _(k):
            inward(k).start()

        if linked:
            carry.start()
            me = Place(dp_size, shard_size)
            total = jnp.sum(gb_in[...], axis=0, keepdims=True)
            total = jnp.broadcast_to(total, (8, 128))
            gb_out[...] = pltpu.roll(total, (128 - me.lane(rows)) % 128, 1)[0:1, :rows]

        @pl.loop(0, steps)
        def _(k):
            pl.when(k >= 2)(lambda: store(k - 2).wait())
            tiles[k % 2] = dot(links[k // per_cluster], spread[place(k)], NN)
            store(k).start()
            inward(k).wait()
            outward(k).start()

        @pl.loop(0, steps)
        def _(k):
            outward(k).wait()

        for k in (steps - 2, steps - 1):
            store(k).wait()
        if linked:
            carry.wait()

    away = pl.BlockSpec(memory_space=pltpu.HBM)
    here = pl.BlockSpec(memory_space=pltpu.VMEM)
    return pl.pallas_call(
        kernel,
        out_shape=(
            jax.ShapeDtypeStruct((nodes, width), F32),
            jax.ShapeDtypeStruct((nodes, width), BF16),
            jax.ShapeDtypeStruct((rows, width), F32),
            jax.ShapeDtypeStruct((1, rows), F32),
        ),
        in_specs=[here, here, away, here, here],
        out_specs=(away, away, away, here),
        scratch_shapes=[
            pltpu.VMEM((steps, part_rows, width), BF16),
            pltpu.VMEM((2, CLUSTER, PC), F32),
            pltpu.SemaphoreType.DMA((2 * steps + 3,)),
        ],
        compiler_params=pltpu.CompilerParams(vmem_limit_bytes=14 * 2**20),
        name="features",
    )


def solution(mesh):
    dp_size, shard_size = mesh.shape["dp"], mesh.shape["shard"]

    def keep(array):
        return pltpu.with_memory_space_constraint(array, pltpu.VMEM)

    def leave(array):
        return pltpu.with_memory_space_constraint(array, pltpu.HBM)

    def on_device(features, neighbors, weight, bias_terms, grad_out):
        nodes, width = features.shape
        rows = weight.shape[0]
        layer = make_kernel(dp_size, shard_size, rows, width, nodes)
        last = make_last(dp_size, shard_size, rows, width, nodes)
        if linkable(rows):
            act, spread, links, grad_weight, bias_sums = layer(
                features, neighbors, weight, bias_terms.reshape(1, rows), grad_out
            )
            grad_features, output, grad_weight, grad_bias = last(
                keep(links), keep(spread), leave(act), keep(grad_weight), keep(bias_sums)
            )
            return output, grad_features, grad_weight, grad_bias.reshape(rows)
        both = ("dp", "shard")
        full = lax.all_gather(weight, both, axis=0, tiled=True)
        bias = lax.all_gather(bias_terms, both, axis=0, tiled=True).astype(F32)
        act, spread, links, parts, bias_sums = layer(
            features,
            neighbors,
            full.reshape(dp_size // 4, 2, 2, shard_size * rows, width),
            jnp.broadcast_to(bias, (8, width)),
            grad_out,
        )
        grad_features, output, *_ = last(
            keep(links),
            keep(spread),
            leave(act),
            jnp.zeros((rows, width), F32),
            jnp.zeros((8, 128), F32),
        )
        parts = parts.reshape(width, width).astype(F32)
        bias_sums = jnp.sum(bias_sums, axis=0)
        return (
            output,
            grad_features,
            lax.psum_scatter(parts, both, scatter_dimension=0, tiled=True),
            lax.psum_scatter(bias_sums, both, scatter_dimension=0, tiled=True),
        )

    split = P(("dp", "shard"), None)
    flat = P(("dp", "shard"))
    return jax.shard_map(
        on_device,
        mesh=mesh,
        in_specs=(split, split, split, flat, split),
        out_specs=(split, split, split, flat),
        check_vma=False,
    )
```

profile of v0, /device:TPU:0, one launch (start us, length us, event | category | flops | bytes accessed | tf_op | source)
XLA Modules:
  0.0 144.5 jit_solution(9618230830126463407)
XLA Ops:
  0.6 130.9 %layer.1 = (bf16[2048,2048]{1,0:T(8,128)(2,1)}, bf16[2048,2048]{1,0:T(8,128)(2,1)S(1)}, bf16[2,1024,1024]{2,1,0:T(8,128)(2,1)S(1)}, f32[64,2048]{1,0:T(8,128)S(1)}, f32[8,128]{1,0:T(8,128)S(1)}) custom-call(bf16[2048,2048]{1,0:T(8,128)(2,1)} %f_hbm.1, s32[2048,128]{1,0:T(8,128)} %n_hbm.1, bf16[64,2048]{1,0:T(8,128)(2,1)} %w_hbm.1, bf16[1,64]{1,0:T(2,128)(2,1)} %bitcast.2, ...), custom_call_target="tpu_custom_call" | custom-call | tf_op jit(solution)/shard_map/layer/pallas_call | solution.py:844
  131.6 12.9 %features.1 = (f32[2048,2048]{1,0:T(8,128)}, bf16[2048,2048]{1,0:T(8,128)(2,1)}, f32[64,2048]{1,0:T(8,128)}, f32[1,64]{1,0:T(1,128)}) custom-call(bf16[2,1024,1024]{2,1,0:T(8,128)(2,1)S(1)} %get-tuple-element.13.links, bf16[2048,2048]{1,0:T(8,128)(2,1)S(1)} %get-tuple-element.14.spread, bf16[2048,2048]{1,0:T(8,128)(2,1)} %get-tuple-element.15.act_in, ...), custom_call_target="tpu_custom_call" | custom-call | tf_op jit(solution)/shard_map/features/pallas_call | solution.py:847
where the time goes:
time: 145 us; the launch traced here: 144 us
  Pallas kernels  144 us (99%)
    pallas_call x1, Pallas kernels, on_device(): layer(features, neighbors, weight, bias_terms.reshape(1, rows), grad_out)  131 us
    pallas_call x1, Pallas kernels, on_device(): last(keep(links), keep(spread), leave(act), keep(grad_weight), keep(bias_...  12.9 us

commit v1 on v0

--- a/solution.py
+++ b/solution.py
@@ -39,25 +39,20 @@
 )
 PANEL_GATHER = (
     (0, "ready", 1),
-    (1, "pass", 2),
-    (4, "pass", 3),
+    (3, "pass", 2),
     (4, "ready", 2),
+    (6, "pass", 3),
     (8, "ready", 3),
 )
-PANEL_SCATTER = (
-    (7, 1, 0),
-    (11, 1, 1),
-    (13, 2, 0),
-    (14, 2, 1),
-    (15, 1, 2),
-)
+PANEL_SCATTER = ((9, 1, 0), (13, 1, 1), (15, 2, 0), (17, 2, 1))
 BACK_SCATTER = (
     (0, 3, 0),
-    (1, 3, 1),
-    (1, 2, 2),
-    (3, 1, 3),
-    (3, 3, 2),
-    (5, 2, 3),
+    (0, 1, 2),
+    (2, 3, 1),
+    (3, 2, 2),
+    (4, 1, 3),
+    (6, 3, 2),
+    (6, 2, 3),
 )
 
 
@@ -115,11 +110,10 @@
         path = SCATTER[0] if t == "bias" else SCATTER[t]
         for k in range(3):
             for o in range(1, sizes[path[k]]):
-                for h in range(2 if k == 0 and path[0] == "x" else 1):
-                    sems["scatter", t, k, o, h]
+                sems["scatter", t, k, o]
     sems["swap", "bias"]
-    for s in range(len(SCATTER)):
-        sems["swap", s]
+    for j in range(len(SCATTER) // 2):
+        sems["swap", j]
     return sems
 
 
@@ -390,21 +384,13 @@
             for at, kind, panel in MIX_EVENTS:
                 pl.when(s == at)(lambda k=kind, p=panel: gather_event(k, p))
 
-        half_y = Y // 2
-        y_half = y // half_y
-
-        def half_of(hh):
-            if isinstance(hh, int):
-                return y_half if hh else 1 - y_half
-            return jnp.where(hh == 0, 1 - y_half, y_half)
-
-        def part(pt, t, core, **at):
+        def part(pt, t, **at):
             ys, xs = at.get("y", ALL), at.get("x", ALL)
             if t == "bias":
                 zs = pl.ds(at["z"], 1) if "z" in at else ALL
-                return ptb.at[ys, xs, core, zs]
+                return ptb.at[ys, xs, c, zs]
             zs = pl.ds(pl.multiple_of(at["z"] * R, R), R) if "z" in at else ALL
-            return pt.at[t // 2, ys, xs, core, zs, pl.ds(t % 2 * HC, HC)]
+            return pt.at[t // 2, ys, xs, zs, pl.ds(t % 2 * HC, HC)]
 
         def scatter_path(t):
             return SCATTER[0] if t == "bias" else SCATTER[t]
@@ -412,32 +398,20 @@
         def landing(t, k):
             return stage[(len(SCATTER) if t == "bias" else t) * 3 + k]
 
-        def scatter_send(pt, t, k, h=None):
+        def scatter_send(pt, t, k):
             path = scatter_path(t)
 
             def make(o):
                 at = fixed(path[:k])
                 at[path[k]] = me.shifted(path[k], o)
-                dst = landing(t, k).at[o - 1]
-                if h is not None:
-                    ys = pl.ds(half_of(h) * half_y, half_y)
-                    at["y"] = ys
-                    dst = dst.at[ys]
-                return part(pt, t, c, **at), dst, me.peer(path[k], o)
+                return part(pt, t, **at), landing(t, k).at[o - 1], me.peer(path[k], o)
 
             for o in me.offsets(path[k]):
-                send(("scatter", t, k, o, h or 0), lambda o=o: make(o))
+                send(("scatter", t, k, o), lambda o=o: make(o))
 
         def scatter_wait(t, k):
-            path = scatter_path(t)
-            for o in me.offsets(path[k]):
-                ref = landing(t, k).at[o - 1]
-                if t != "bias" and k == 0 and path[0] == "x":
-                    for i in range(2):
-                        ys = pl.ds(half_of(i) * half_y, half_y)
-                        arrived(("scatter", t, k, o, i), ref.at[ys])
-                else:
-                    arrived(("scatter", t, k, o, 0), ref)
+            for o in me.offsets(scatter_path(t)[k]):
+                arrived(("scatter", t, k, o), landing(t, k).at[o - 1])
 
         def over_rows(shape, action):
             lead, high = shape[:-2], shape[-2]
@@ -462,7 +436,7 @@
 
         def scatter_add(pt, t, k):
             path = scatter_path(t)
-            mine = part(pt, t, c, **fixed(path[: k + 1]))
+            mine = part(pt, t, **fixed(path[: k + 1]))
             others = [landing(t, k).at[o - 1] for o in me.offsets(path[k])]
             if t == "bias":
                 total = mine[...]
@@ -485,33 +459,13 @@
 
             over_rows(mine.shape, piece)
 
-        def swap(pt, s):
-            j, hh = s // 2, s % 2
-            ys = pl.ds(half_of(hh) * half_y, half_y)
-            i = sems["swap", 0] + s
+        def swap(po, j):
+            i = sems["swap", 0] + j
             return pltpu.make_async_remote_copy(
-                src_ref=pt.at[j, ys, :, 1 - c], dst_ref=cr.at[j, ys],
+                src_ref=po.at[j], dst_ref=cr.at[j],
                 send_sem=ssem.at[i], recv_sem=rsem.at[i],
                 device_id=me.peer("c", 1), device_id_type=MESH,
             )
-
-        def core_sum(pt, s):
-            swap(pt, s).wait_recv()
-            ys = pl.ds(half_of(s % 2) * half_y, half_y)
-            mine, other = pt.at[s // 2, ys, :, c], cr.at[s // 2, ys]
-
-            def piece(at):
-                mine[at] = (mine[at].astype(F32) + other[at].astype(F32)).astype(BF16)
-
-            over_rows(mine.shape, piece)
-
-        def first_sends(pt, s):
-            j, hh = s // 2, s % 2
-            for t in (2 * j, 2 * j + 1):
-                if scatter_path(t)[0] == "x":
-                    scatter_send(pt, t, 0, hh)
-                elif hh == (0 if Y == 2 else 1):
-                    scatter_send(pt, t, 0)
 
         def scatter_event(pt, k, j):
             ts = (2 * j, 2 * j + 1) + (("bias",) if j == panels - 1 else ())
@@ -521,16 +475,15 @@
                 if k < 3:
                     scatter_send(pt, t, k)
 
-        def store_part(pt, s):
-            j, hh = s // 2, s % 2
-            ys = pl.ds(half_of(hh) * half_y, half_y)
+        def store_part(held, j, core, k):
+            col = pl.ds(pl.multiple_of(j * PC, PC), PC)
             return pltpu.make_async_copy(
-                pt.at[j, ys],
-                gw_out.at[ys, :, :, :, pl.ds(pl.multiple_of(j * PC, PC), PC)],
-                lsem.at[12 + panels + s],
+                held.at[j],
+                gw_out.at[:, :, core, :, col],
+                lsem.at[12 + (1 + k) * panels + j],
             )
 
-        def panel_phase(pt, acc_a, acc_b, go, ac):
+        def panel_phase(pt, po, acc_a, acc_b, go, ac):
             def tile_rows(i):
                 return pl.ds(pl.multiple_of(i * TM, TM), TM)
 
@@ -545,35 +498,31 @@
                     ac.at[i], block(act_hbm, j, i), lsem.at[4 + i]
                 )
 
-            def product(j, i):
-                panel = wg[j].reshape(width, PC)
+            def product(j, i, cols):
+                panel = wg[j, :, :, :, :, cols].reshape(width, HC)
                 return dot(mixed[tile_rows(i), :], panel, NN)
 
-            def finish(acc, j, i):
+            def finish(acc, j, i, cols):
                 r = tile_rows(i)
-                col = pl.ds(pl.multiple_of(j * PC, PC), PC)
-                v = acc[...] + brow[0:1, col]
+                col = pl.ds(pl.multiple_of(j * PC + cols.start, HC), HC)
+                v = acc[:, cols] + brow[0:1, col]
                 u = v * v
                 h = 0.5 + 0.5 * jnp.tanh(v * (ALPHA + BETA * u))
                 a = v * h
                 d = h + (a * (1.0 - h)) * (2 * ALPHA + (6 * BETA) * u)
-                g = go[i].astype(F32) * d
-                ac[i] = a.astype(BF16)
+                g = go[i, :, cols].astype(F32) * d
+                ac[i, :, cols] = a.astype(BF16)
                 fg[r, col] = g.astype(BF16)
-                gbacc[:, col] += jnp.sum(g.reshape(TM // 8, 8, PC), axis=0)
-
-            def weight_tile(j, hh):
-                h = half_of(hh)
-                rows_ = pl.ds(pl.multiple_of(h * half_rows, half_rows), half_rows)
+                gbacc[:, col] += jnp.sum(g.reshape(TM // 8, 8, HC), axis=0)
+
+            def weight_rows(j, core):
+                lhs = [
+                    mixed[:, pl.ds(pl.multiple_of((b * 2 + core) * SR, SR), SR)]
+                    for b in range(Y * X)
+                ]
                 col = pl.ds(pl.multiple_of(j * PC, PC), PC)
-                total = dot(mixed[:, rows_], fg[:, col], TN).astype(BF16)
-                pt[j, pl.ds(h * half_y, half_y)] = total.reshape(half_y, X, 2, SR, PC)
-
-            def leave(j, hh):
-                if linked:
-                    swap(pt, 2 * j + hh).start()
-                else:
-                    store_part(pt, 2 * j + hh).start()
+                total = dot(jnp.concatenate(lhs, axis=1), fg[:, col], TN)
+                return total.reshape(Y, X, SR, PC)
 
             def events(step):
                 for at, kind, panel in PANEL_GATHER:
@@ -582,16 +531,6 @@
                     return
                 for at, k, panel in PANEL_SCATTER:
                     pl.when(step == at)(lambda k=k, p=panel: scatter_event(pt, k, p))
-
-            def core_step(e, when):
-                if not linked:
-                    return
-
-                @pl.when(when)
-                def _():
-                    core_sum(pt, e)
-                    for fixed_e in range(2 * panels - 1):
-                        pl.when(e == fixed_e)(lambda k=fixed_e: first_sends(pt, k))
 
             def send_bias():
                 for d in range(n_dev):
@@ -609,37 +548,56 @@
                 mine[...] = mine[...] + crb[...]
                 scatter_send(pt, "bias", 0)
 
+            def pair(j, h):
+                for k in range(2):
+                    load_g(j, 2 * h + k).wait()
+                    pl.when(j > 0)(lambda i=2 * h + k: store_act(j - 1, i).wait())
+                for k, acc, other in ((0, acc_a, acc_b), (1, acc_b, acc_a)):
+                    i = 2 * h + k
+                    n = jnp.minimum(j * per_panel + i + 1, tiles - 1)
+                    for q in range(PC // HC):
+                        cols = pl.ds(q * HC, HC)
+                        other[:, cols] = product(n // per_panel, n % per_panel, cols)
+                        finish(acc, j, i, cols)
+                for k in range(2):
+                    i = 2 * h + k
+                    store_act(j, i).start()
+                    pl.when(j < panels - 1)(lambda i=i: load_g(j + 1, i).start())
+
+            def own_rows(j):
+                total = weight_rows(j, c)
+                if linked:
+                    swap(po, j).wait_recv()
+                    total = total + cr[j].astype(F32)
+                pt[j] = total.astype(BF16)
+                if not linked:
+                    store_part(pt, j, c, 0).start()
+                    return
+                for p in range(panels):
+
+                    @pl.when(j == p)
+                    def _():
+                        for t in (2 * p, 2 * p + 1):
+                            scatter_send(pt, t, 0)
+                        if p == panels - 1:
+                            sum_bias()
+
+            def other_rows(j):
+                po[j] = weight_rows(j, 1 - c).astype(BF16)
+                if linked:
+                    swap(po, j).start()
+                    pl.when(j == panels - 1)(send_bias)
+                else:
+                    store_part(po, j, 1 - c, 1).start()
+
             def panel(j):
-                final = panels - 1
-
-                @pl.loop(0, per_panel // 2)
+                @pl.loop(0, 2)
                 def _(h):
-                    for k, acc, other in ((0, acc_a, acc_b), (1, acc_b, acc_a)):
-                        i = 2 * h + k
-                        load_g(j, i).wait()
-                        pl.when(j > 0)(lambda i=i: store_act(j - 1, i).wait())
-                    for k, acc, other in ((0, acc_a, acc_b), (1, acc_b, acc_a)):
-                        i = 2 * h + k
-                        n = jnp.minimum(j * per_panel + i + 1, tiles - 1)
-                        other[...] = product(n // per_panel, n % per_panel)
-                        finish(acc, j, i)
-                    for k in range(2):
-                        i = 2 * h + k
-                        store_act(j, i).start()
-                        pl.when(j < final)(lambda i=i: load_g(j + 1, i).start())
-                    core_step(2 * j - 1, (h == 0) & (j > 0))
-                    events(4 * j + h)
-
-                @pl.loop(0, 2)
-                def _(hh):
-                    if linked:
-                        pl.when((j == final) & (hh == 0))(send_bias)
-                    weight_tile(j, hh)
-                    leave(j, hh)
-                    if linked:
-                        pl.when((j == final) & (hh == 1))(sum_bias)
-                    core_step(2 * j, hh == 1)
-                    events(4 * j + 2 + hh)
+                    pl.when(j < panels)(lambda: pair(j, h))
+                    events(4 * j + 2 * h)
+                    pl.when((h == 0) & (j > 0))(lambda: own_rows(j - 1))
+                    pl.when((h == 1) & (j < panels))(lambda: other_rows(j))
+                    events(4 * j + 2 * h + 1)
 
             for i in range(per_panel):
                 load_g(0, i).start()
@@ -653,12 +611,14 @@
                     tile = tile + bt[d // (X * 2 * S), d // (2 * S) % X, d // S % 2, d % S]
                 brow[:, pl.ds(k * 128, 128)] = tile
             gbacc[...] = jnp.zeros_like(gbacc)
-            acc_a[...] = product(0, 0)
-            pl.loop(0, panels)(panel)
+            for q in range(PC // HC):
+                cols = pl.ds(q * HC, HC)
+                acc_a[:, cols] = product(0, 0, cols)
+            pl.loop(0, panels + 1)(panel)
             for i in range(per_panel):
                 store_act(panels - 1, i).wait()
 
-        def back_phase(pt):
+        def back_phase(pt, po):
             steps = nodes // BM
 
             @pl.loop(0, steps)
@@ -674,34 +634,30 @@
                 if not linked:
                     return
 
-                @pl.when(s == 0)
-                def _():
-                    core_sum(pt, 2 * panels - 1)
-                    first_sends(pt, 2 * panels - 1)
-
                 for at, k, panel in BACK_SCATTER:
                     pl.when(s == at)(lambda k=k, p=panel: scatter_event(pt, k, p))
 
             if linked:
                 scatter_event(pt, 3, panels - 1)
-                for s in range(2 * panels):
-                    swap(pt, s).wait_send()
+                for j in range(panels):
+                    swap(po, j).wait_send()
                 for name, make in started.items():
                     remote(name, *make()).wait_send()
             else:
-                for s in range(2 * panels):
-                    store_part(pt, s).wait()
+                for j in range(panels):
+                    store_part(pt, j, c, 0).wait()
+                    store_part(po, j, 1 - c, 1).wait()
                 gb_out[...] = gbacc[...]
 
-        def with_parts(pt):
+        def with_parts(pt, po):
             pl.run_scoped(
-                lambda *refs: panel_phase(pt, *refs),
+                lambda *refs: panel_phase(pt, po, *refs),
                 *[pltpu.VMEM((TM, PC), F32)] * 2,
                 *[pltpu.VMEM((per_panel, TM, PC), BF16)] * 2,
             )
-            back_phase(pt)
-
-        pl.run_scoped(with_parts, pltpu.VMEM((panels, Y, X, 2, SR, PC), BF16))
+            back_phase(pt, po)
+
+        pl.run_scoped(with_parts, *[pltpu.VMEM((panels, Y, X, SR, PC), BF16)] * 2)
 
     away = pl.BlockSpec(memory_space=pltpu.HBM)
     here = pl.BlockSpec(memory_space=pltpu.VMEM)

time: 145 us -> 142 us (0.979)
  Pallas kernels: 144 us -> 141 us
    pallas_call x1, Pallas kernels: 131 us -> 128 us  [on_device(): layer(features, neighbors, weight, bias_terms.reshape(1, rows), grad_out)]
where the time goes in v1:
time: 142 us; the launch traced here: 141 us
  Pallas kernels  141 us (99%)
    pallas_call x1, Pallas kernels, on_device(): layer(features, neighbors, weight, bias_terms.reshape(1, rows), grad_out)  128 us
    pallas_call x1, Pallas kernels, on_device(): last(keep(links), keep(spread), leave(act), keep(grad_weight), keep(bias_...  12.9 us

profile of v1, /device:TPU:0, one launch (start us, length us, event | category | flops | bytes accessed | tf_op | source)
XLA Modules:
  0.0 141.4 jit_solution(4903404219084396544)
XLA Ops:
  0.6 127.6 %layer.1 = (bf16[2048,2048]{1,0:T(8,128)(2,1)}, bf16[2048,2048]{1,0:T(8,128)(2,1)S(1)}, bf16[2,1024,1024]{2,1,0:T(8,128)(2,1)S(1)}, f32[64,2048]{1,0:T(8,128)S(1)}, f32[8,128]{1,0:T(8,128)S(1)}) custom-call(bf16[2048,2048]{1,0:T(8,128)(2,1)} %f_hbm.1, s32[2048,128]{1,0:T(8,128)} %n_hbm.1, bf16[64,2048]{1,0:T(8,128)(2,1)} %w_hbm.1, bf16[1,64]{1,0:T(2,128)(2,1)} %bitcast.2, ...), custom_call_target="tpu_custom_call" | custom-call | tf_op jit(solution)/shard_map/layer/pallas_call | solution.py:800
  128.3 12.9 %features.1 = (f32[2048,2048]{1,0:T(8,128)}, bf16[2048,2048]{1,0:T(8,128)(2,1)}, f32[64,2048]{1,0:T(8,128)}, f32[1,64]{1,0:T(1,128)}) custom-call(bf16[2,1024,1024]{2,1,0:T(8,128)(2,1)S(1)} %get-tuple-element.13.links, bf16[2048,2048]{1,0:T(8,128)(2,1)S(1)} %get-tuple-element.14.spread, bf16[2048,2048]{1,0:T(8,128)(2,1)} %get-tuple-element.15.act_in, ...), custom_call_target="tpu_custom_call" | custom-call | tf_op jit(solution)/shard_map/features/pallas_call | solution.py:803

commit v2 on v1

--- a/solution.py
+++ b/solution.py
@@ -9,10 +9,11 @@
 MESH = pl.DeviceIdType.MESH
 CLUSTER = 1024
 SLOTS = 128
-UNROLL = 32
-LOW = 64
+UNROLL = 64
+LOW = 32
 PC = 512
 HC = 256
+GC = 256
 ALPHA = 0.7978845608028654
 BETA = ALPHA * 0.044715
 NN = (((1,), (0,)), ((), ()))
@@ -499,12 +500,12 @@
                 )
 
             def product(j, i, cols):
-                panel = wg[j, :, :, :, :, cols].reshape(width, HC)
+                panel = wg[j, :, :, :, :, cols].reshape(width, GC)
                 return dot(mixed[tile_rows(i), :], panel, NN)
 
             def finish(acc, j, i, cols):
                 r = tile_rows(i)
-                col = pl.ds(pl.multiple_of(j * PC + cols.start, HC), HC)
+                col = pl.ds(pl.multiple_of(j * PC + cols.start, GC), GC)
                 v = acc[:, cols] + brow[0:1, col]
                 u = v * v
                 h = 0.5 + 0.5 * jnp.tanh(v * (ALPHA + BETA * u))
@@ -513,7 +514,7 @@
                 g = go[i, :, cols].astype(F32) * d
                 ac[i, :, cols] = a.astype(BF16)
                 fg[r, col] = g.astype(BF16)
-                gbacc[:, col] += jnp.sum(g.reshape(TM // 8, 8, HC), axis=0)
+                gbacc[:, col] += jnp.sum(g.reshape(TM // 8, 8, GC), axis=0)
 
             def weight_rows(j, core):
                 lhs = [
@@ -555,8 +556,8 @@
                 for k, acc, other in ((0, acc_a, acc_b), (1, acc_b, acc_a)):
                     i = 2 * h + k
                     n = jnp.minimum(j * per_panel + i + 1, tiles - 1)
-                    for q in range(PC // HC):
-                        cols = pl.ds(q * HC, HC)
+                    for q in range(PC // GC):
+                        cols = pl.ds(q * GC, GC)
                         other[:, cols] = product(n // per_panel, n % per_panel, cols)
                         finish(acc, j, i, cols)
                 for k in range(2):
@@ -611,8 +612,8 @@
                     tile = tile + bt[d // (X * 2 * S), d // (2 * S) % X, d // S % 2, d % S]
                 brow[:, pl.ds(k * 128, 128)] = tile
             gbacc[...] = jnp.zeros_like(gbacc)
-            for q in range(PC // HC):
-                cols = pl.ds(q * HC, HC)
+            for q in range(PC // GC):
+                cols = pl.ds(q * GC, GC)
                 acc_a[:, cols] = product(0, 0, cols)
             pl.loop(0, panels + 1)(panel)
             for i in range(per_panel):

time: 142 us -> 140 us (0.986)
  Pallas kernels: 141 us -> 139 us
    pallas_call x1, Pallas kernels: 128 us -> 126 us  [on_device(): layer(features, neighbors, weight, bias_terms.reshape(1, rows), grad_out)]
where the time goes in v2:
time: 140 us; the launch traced here: 139 us
  Pallas kernels  139 us (99%)
    pallas_call x1, Pallas kernels, on_device(): layer(features, neighbors, weight, bias_terms.reshape(1, rows), grad_out)  126 us
    pallas_call x1, Pallas kernels, on_device(): last(keep(links), keep(spread), leave(act), keep(grad_weight), keep(bias_...  12.9 us

profile of v2, /device:TPU:0, one launch (start us, length us, event | category | flops | bytes accessed | tf_op | source)
XLA Modules:
  0.0 139.4 jit_solution(8101081549908037923)
XLA Ops:
  0.6 125.7 %layer.1 = (bf16[2048,2048]{1,0:T(8,128)(2,1)}, bf16[2048,2048]{1,0:T(8,128)(2,1)S(1)}, bf16[2,1024,1024]{2,1,0:T(8,128)(2,1)S(1)}, f32[64,2048]{1,0:T(8,128)S(1)}, f32[8,128]{1,0:T(8,128)S(1)}) custom-call(bf16[2048,2048]{1,0:T(8,128)(2,1)} %f_hbm.1, s32[2048,128]{1,0:T(8,128)} %n_hbm.1, bf16[64,2048]{1,0:T(8,128)(2,1)} %w_hbm.1, bf16[1,64]{1,0:T(2,128)(2,1)} %bitcast.2, ...), custom_call_target="tpu_custom_call" | custom-call | tf_op jit(solution)/shard_map/layer/pallas_call | solution.py:801
  126.3 12.9 %features.1 = (f32[2048,2048]{1,0:T(8,128)}, bf16[2048,2048]{1,0:T(8,128)(2,1)}, f32[64,2048]{1,0:T(8,128)}, f32[1,64]{1,0:T(1,128)}) custom-call(bf16[2,1024,1024]{2,1,0:T(8,128)(2,1)S(1)} %get-tuple-element.13.links, bf16[2048,2048]{1,0:T(8,128)(2,1)S(1)} %get-tuple-element.14.spread, bf16[2048,2048]{1,0:T(8,128)(2,1)} %get-tuple-element.15.act_in, ...), custom_call_target="tpu_custom_call" | custom-call | tf_op jit(solution)/shard_map/features/pallas_call | solution.py:804

commit v3 on v2

--- a/solution.py
+++ b/solution.py
@@ -34,9 +34,9 @@
 MIX_EVENTS = (
     (0, "third", 1),
     (0, "pass", 0),
-    (3, "third", 2),
-    (7, "third", 3),
-    (7, "pass", 1),
+    (1, "third", 2),
+    (3, "third", 3),
+    (3, "pass", 1),
 )
 PANEL_GATHER = (
     (0, "ready", 1),
@@ -372,16 +372,14 @@
         )
         load_f.wait()
 
-        @pl.loop(0, clusters * 4)
+        @pl.loop(0, clusters * 2)
         def _(s):
-            cl, i, j = s // 4, (s // 2) % 2, s % 2
-            r = pl.ds(pl.multiple_of(cl * CLUSTER + i * 512, 512), 512)
+            cl, j = s // 2, s % 2
             k = pl.ds(pl.multiple_of(cl * CLUSTER, CLUSTER), CLUSTER)
             col = pl.ds(pl.multiple_of(j * half_rows, half_rows), half_rows)
-            links = a2t[cl, :, pl.ds(pl.multiple_of(i * 512, 512), 512)]
-            total = dot(links, fg[k, col], TN)
-            scale = jnp.concatenate([fac[r, :]] * (half_rows // 128), axis=1)
-            mixed[r, col] = (scale * total).astype(BF16)
+            total = dot(a2t[cl], fg[k, col], TN)
+            scale = jnp.concatenate([fac[k, :]] * (half_rows // 128), axis=1)
+            mixed[k, col] = (scale * total).astype(BF16)
             for at, kind, panel in MIX_EVENTS:
                 pl.when(s == at)(lambda k=kind, p=panel: gather_event(k, p))
 

time: 140 us -> 140 us (level)
  no operation moved by 1% of the time
where the time goes in v3:
time: 140 us
  Pallas kernels  139 us (99%)
    pallas_call x1, Pallas kernels, on_device(): layer(features, neighbors, weight, bias_terms.reshape(1, rows), grad_out)  126 us
    pallas_call x1, Pallas kernels, on_device(): last(keep(links), keep(spread), leave(act), keep(grad_weight), keep(bias_...  12.9 us

profile of v3, /device:TPU:0, one launch (start us, length us, event | category | flops | bytes accessed | tf_op | source)
XLA Modules:
  0.0 139.6 jit_solution(14113042552235615840)
XLA Ops:
  0.6 125.9 %layer.1 = (bf16[2048,2048]{1,0:T(8,128)(2,1)}, bf16[2048,2048]{1,0:T(8,128)(2,1)S(1)}, bf16[2,1024,1024]{2,1,0:T(8,128)(2,1)S(1)}, f32[64,2048]{1,0:T(8,128)S(1)}, f32[8,128]{1,0:T(8,128)S(1)}) custom-call(bf16[2048,2048]{1,0:T(8,128)(2,1)} %f_hbm.1, s32[2048,128]{1,0:T(8,128)} %n_hbm.1, bf16[64,2048]{1,0:T(8,128)(2,1)} %w_hbm.1, bf16[1,64]{1,0:T(2,128)(2,1)} %bitcast.2, ...), custom_call_target="tpu_custom_call" | custom-call | tf_op jit(solution)/shard_map/layer/pallas_call | solution.py:799
  126.5 12.9 %features.1 = (f32[2048,2048]{1,0:T(8,128)}, bf16[2048,2048]{1,0:T(8,128)(2,1)}, f32[64,2048]{1,0:T(8,128)}, f32[1,64]{1,0:T(1,128)}) custom-call(bf16[2,1024,1024]{2,1,0:T(8,128)(2,1)S(1)} %get-tuple-element.13.links, bf16[2048,2048]{1,0:T(8,128)(2,1)S(1)} %get-tuple-element.14.spread, bf16[2048,2048]{1,0:T(8,128)(2,1)} %get-tuple-element.15.act_in, ...), custom_call_target="tpu_custom_call" | custom-call | tf_op jit(solution)/shard_map/features/pallas_call | solution.py:802
